TPU v7x, 256 devices: a whole 4x4x8 slice. The times are simulated.
256 devices in a mesh: dom: 256 (over z, x, y, core).
Axes of the slice: x: 4, y: 4, z: 8, core: 2. Of those that a mesh axis runs over, the one named last changes fastest.
Arguments:
- coef_init: float32 [1024, 128], P('dom'), may hold values from -6 to 6
- basis: bfloat16 [393216, 1024], P('dom'), may hold values from -0.75 to 0.75
- basis_scale: float32 [3072], P('dom'), may hold values from 0.5 to 2
- ext_force: float32 [393216, 128], P('dom'), may hold values from -6 to 6
- precond: float32 [1024], P('dom'), may hold values from 0.5 to 6, as said below
- connectivity: int32 [115200, 8], P('dom'), may hold values from 0 to 767, as said below
- halo_nodes: int32 [65536], P('dom'), may hold values from 0 to 511, as said below
- plastic: int32 [115200], P('dom'), may hold values 0 or 1
Outputs:
- coef_final: float32 [1024, 128], P('dom')
- nodal_residual: float32 [393216, 128], P('dom')
Inputs may be any that keep to these rules, and one draw needn't show every extreme that they name: `connectivity`: each part is a structured block of 16 x 16 x 2 nodes, numbered in a part-specific order; each row lists an element's 8 corners in corner-bit order (bit 0 along x, bit 1 along y, bit 2 along z). Entries below 512 are the part's own nodes; an entry 512 + h names the node listed h-th in the next part's halo_nodes (the next part's first z layer). `halo_nodes`: the entries of one part are its own local node numbers of its first z layer, in grid order with x fastest, all distinct. `precond`: Positive.
All inputs are finite; a program needn't handle non-finite values. No bound on the sum of `plastic` on one device may be relied on, other than what follows from the above.
Results may differ from a plain program's by a relative error of at most 0.0087.
Values may be sent and summed in bfloat16 or wider, within the bound.
A program may use at most 64 MiB of HBM per device.

v0:
```python
import jax
import jax.numpy as jnp
from jax import lax
from jax.sharding import PartitionSpec as P

R = 1024
ITERS = 2
STEP_SIZE = 0.5
SHEAR_MODULUS = 1.0
LAME_FIRST = 1.5
HARDENING = 0.5
YIELD_STRESS = 3.0
EPSILON = 1e-05


def from_behind(value, axis, steps):
    count = lax.axis_size(axis)
    leading, last = (max(0, -steps), min(count, count - steps))
    return lax.ppermute(value, axis, [(source, source + steps) for source in range(leading, last)])


def corner_table():
    corner_bits = jnp.arange(8)[:, None] >> jnp.arange(3)[None, :] & 1
    return (2.0 * corner_bits.astype(jnp.float32) - 1.0) / 4.0


def element_forces(corner_disp, flags, corners):
    gradient = jnp.einsum("eaic,aj->eijc", corner_disp, corners, precision=lax.Precision.HIGHEST)
    strain = 0.5 * (gradient + jnp.swapaxes(gradient, 1, 2))
    volumetric = strain[:, 0, 0] + strain[:, 1, 1] + strain[:, 2, 2]
    identity = jnp.eye(3, dtype=jnp.float32)[None, :, :, None]
    shear_part = 2.0 * SHEAR_MODULUS * (strain - volumetric[:, None, None] / 3.0 * identity)
    magnitude = jnp.sqrt(jnp.sum(shear_part * shear_part, axis=(1, 2)))
    total_modulus = 2.0 * SHEAR_MODULUS + HARDENING
    plastic_factor = HARDENING / total_modulus + 2.0 * SHEAR_MODULUS * YIELD_STRESS / (
        total_modulus * jnp.maximum(magnitude, YIELD_STRESS)
    )
    factor = jnp.where(flags[:, None] == 1, plastic_factor, jnp.ones_like(plastic_factor))
    stress = LAME_FIRST * volumetric[:, None, None] * identity + factor[:, None, None] * shear_part
    return jnp.einsum("eijc,aj->eaic", stress, corners, precision=lax.Precision.HIGHEST)


def apply_scale(values, scales):
    return (values.reshape(scales.shape[0], -1, values.shape[-1]) * scales[:, None, None]).reshape(
        values.shape
    )


def on_device(coef_init, basis, basis_scale, ext_force, precond, connectivity, halo_nodes, plastic):
    rows_dev, cases = ext_force.shape
    node_count = rows_dev // 3
    halo_count = halo_nodes.shape[0]
    corners = corner_table()
    node_ids = jnp.arange(node_count + halo_count, dtype=jnp.int32)
    incidence = (node_ids[:, None] == connectivity.reshape(-1)[None, :]).astype(jnp.float32)
    nodal_residual = ext_force
    coef_out = coef_init
    for sweep in range(ITERS):
        lifted = jnp.dot(
            basis,
            lax.all_gather(coef_out.astype(jnp.bfloat16), "dom", axis=0, tiled=True),
            preferred_element_type=jnp.float32,
        )
        nodes = apply_scale(lifted, basis_scale).reshape(node_count, 3, cases)
        outgoing = nodes[halo_nodes]
        residual_incoming = from_behind(outgoing, "dom", -1)
        extended = jnp.concatenate([nodes, residual_incoming], axis=0)
        corner_force = element_forces(extended[connectivity], plastic, corners)
        internal = jnp.dot(
            incidence,
            corner_force.reshape(-1, 3 * cases),
            precision=lax.Precision.HIGHEST,
            preferred_element_type=jnp.float32,
        ).reshape(node_count + halo_count, 3, cases)
        returned = from_behind(internal[node_count:], "dom", 1)
        own_force = internal[:node_count].at[halo_nodes].add(returned)
        nodal_residual = ext_force - own_force.reshape(rows_dev, cases)
        scaled = apply_scale(nodal_residual, basis_scale).astype(jnp.bfloat16)
        reduced = lax.psum_scatter(
            lax.dot_general(
                basis, scaled, (((0,), (0,)), ((), ())), preferred_element_type=jnp.float32
            ),
            "dom",
            scatter_dimension=0,
            tiled=True,
        )
        update = precond[:, None] * reduced
        squares = lax.psum(jnp.sum(update * update, axis=0), "dom")
        root_mean = jnp.sqrt(squares / R + EPSILON)
        coef_out = coef_out + STEP_SIZE * update / root_mean
    return (coef_out, nodal_residual)


def solution(mesh):
    return jax.shard_map(
        on_device,
        mesh=mesh,
        in_specs=(
            P("dom", None),
            P("dom", None),
            P("dom"),
            P("dom", None),
            P("dom"),
            P("dom", None),
            P("dom"),
            P("dom"),
        ),
        out_specs=(P("dom", None), P("dom", None)),
        check_vma=False,
    )
```

profile of v0, /device:TPU:1, one launch (start us, length us, event | category | flops | bytes accessed | tf_op | source)
XLA Modules:
  0.0 1042.2 jit_solution(15831920046400500216)
XLA Ops:
  9.8 67.0 %all-gather = bf16[256,4,128]{2,1,0:T(4,128)(2,1)S(1)} all-gather(bf16[1,4,128]{2,1,0:T(4,128)(2,1)S(1)} %convert_bitcast_fusion.1), channel_id=1, replica_groups=mesh['dom'=256] {'dom'}, dimensions={0}, use_global_device_ids=true | all-gather | bytes 263168 | tf_op jit(solution)/shard_map/all_gather | solution.py:61
  78.7 2.3 reshape.92
  81.0 2.8 broadcast_multiply_fusion.1
  83.8 3.0 gather_fusion
  92.8 4.8 collective-permute-done
  97.6 3.0 pad_maximum_fusion
  100.6 14.1 %gather_fusion.1 = f32[3600,3,128]{2,1,0:T(4,128)} fusion(f32[768,3,128]{2,1,0:T(4,128)} %pad_maximum_fusion, s32[4096]{0:T(1024)S(1)} %pad_clamp_fusion), kind=kCustom, calls=%fused_computation.1 | custom fusion | bytes 11073600 | tf_op jit(solution)/shard_map/gather | solution.py:68
  114.7 8.2 fusion.6
  127.3 4.6 multiply_add_fusion.1
  131.9 6.6 convolution_bitcast_fusion.1
  138.4 8.3 fusion.1
  154.6 2.5 copy.44
  158.9 26.5 %scatter_fusion = f32[512,3,128]{2,1,0:T(4,128)} fusion(f32[512,3,128]{2,1,0:T(4,128)} %copy.44, s32[256]{0:T(256)S(1)} %compare_select_fusion.1, f32[256,3,128]{2,1,0:T(4,128)} %collective-permute-done.1), kind=kCustom, calls=%fused_computation.4 | custom fusion | flops 98304 | bytes 1180672 | tf_op jit(solution)/shard_map/scatter-add | solution.py:76
  187.7 3.2 convolution_bitcast_fusion.4
  191.1 253.2 %all-reduce.5.cloned.1.call-done = f32[1024,128]{0,1:T(8,128)} async-done(((f32[1024,128]{0,1:T(8,128)}), f32[1024,128]{0,1:T(8,128)}) %all-reduce.5.cloned.1.call-update) | async-done | bytes 524304
  445.4 77.5 %psum.14 = f32[128]{0:T(128)S(1)} all-reduce(f32[128]{0:T(128)S(1)} %multiply_reduce_fusion.3), channel_id=1, replica_groups=mesh['dom'=256] {'dom'}, use_global_device_ids=true, to_apply=%region_4.5 | all-reduce | flops 128 | bytes 1024 | tf_op jit(solution)/shard_map/psum | solution.py:88
  524.4 58.8 %all-gather.1 = bf16[256,4,128]{2,1,0:T(4,128)(2,1)S(1)} all-gather(bf16[1,4,128]{2,1,0:T(4,128)(2,1)S(1)} %copy.46), channel_id=1, replica_groups=mesh['dom'=256] {'dom'}, dimensions={0}, use_global_device_ids=true | all-gather | bytes 263168 | tf_op jit(solution)/shard_map/all_gather | solution.py:61
  585.3 2.3 copy.47
  587.7 2.3 reshape.95
  590.0 2.8 broadcast_multiply_fusion
  592.8 3.0 gather_fusion.2
  597.8 8.7 collective-permute-done.2
  606.6 2.8 pad_maximum_fusion.1
  609.4 14.1 %gather_fusion.3 = f32[3600,3,128]{2,1,0:T(4,128)} fusion(f32[768,3,128]{2,1,0:T(4,128)} %pad_maximum_fusion.1, s32[4096]{0:T(1024)S(1)} %pad_clamp_fusion), kind=kCustom, calls=%fused_computation.3 | custom fusion | bytes 11073600 | tf_op jit(solution)/shard_map/gather | solution.py:68
  623.5 8.2 fusion.4
  636.0 4.6 multiply_add_fusion
  640.6 6.6 convolution_bitcast_fusion
  647.2 8.3 fusion
  661.5 2.5 copy.53
  665.9 26.5 %scatter_fusion.1 = f32[512,3,128]{2,1,0:T(4,128)} fusion(f32[512,3,128]{2,1,0:T(4,128)} %copy.53, s32[256]{0:T(256)S(1)} %compare_select_fusion.1, f32[256,3,128]{2,1,0:T(4,128)} %collective-permute-done.3), kind=kCustom, calls=%fused_computation.5 | custom fusion | flops 98304 | bytes 1180672 | tf_op jit(solution)/shard_map/scatter-add | solution.py:76
  698.9 256.0 %all-reduce.7.cloned.1.call-done = f32[1024,128]{0,1:T(8,128)} async-done(((f32[1024,128]{0,1:T(8,128)}), f32[1024,128]{0,1:T(8,128)}) %all-reduce.7.cloned.1.call-update) | async-done | bytes 524304
  955.9 77.5 %psum.15 = f32[128]{0:T(128)S(1)} all-reduce(f32[128]{0:T(128)S(1)} %multiply_reduce_fusion.2), channel_id=1, replica_groups=mesh['dom'=256] {'dom'}, use_global_device_ids=true, to_apply=%region_9.10 | all-reduce | flops 128 | bytes 1024 | tf_op jit(solution)/shard_map/psum | solution.py:88
  (88 shorter events, 54.7 us)
Async XLA Ops:
  7.2 69.6 %copy-start = (bf16[1536,1024]{1,0:T(8,128)(2,1)S(1)}, bf16[1536,1024]{1,0:T(8,128)(2,1)}, u32[]{:S(2)}) copy-start(bf16[1536,1024]{1,0:T(8,128)(2,1)} %param.9) | copy-start | bytes 9437188
  7.2 437.2 %all-reduce.5.cloned.1.call-start = ((), (), s32[]{:S(2)}) async-start(), calls=%async_computation | async-start | bytes 1048576
  78.7 10.2 copy-start.6
  78.7 14.1 %copy-start.14 = (s32[450]{0:T(512)S(1)}, s32[450]{0:T(512)}, u32[]{:S(2)}) copy-start(s32[450]{0:T(512)} %param.15) | copy-start | bytes 5404
  86.8 10.8 %collective-permute-start = (f32[256,3,128]{2,1,0:T(4,128)}, f32[256,3,128]{2,1,0:T(4,128)}, u32[]{:S(2)}, u32[]{:S(2)}) collective-permute-start(f32[256,3,128]{2,1,0:T(4,128)} %gather_fusion), channel_id=1, source_target_pairs={{1,0},{2,1},{3,2},{4,3},{5,4},{6,5},{7,6},{8,7},{9,8},{10,9},{11,1... | collective-permute-start | bytes 1179656 | tf_op jit(solution)/shard_map/ppermute | solution.py:19
  92.7 45.7 %copy-start.7 = (s32[3600]{0:T(1024)}, s32[3600]{0:T(1024)S(1)}, u32[]{:S(2)}) copy-start(s32[3600]{0:T(1024)S(1)} %eq.35) | copy-start | bytes 43204
  138.4 14.0 %copy-start.13 = (f32[12]{0:T(128)S(1)}, f32[12]{0:T(128)}, u32[]{:S(2)}) copy-start(f32[12]{0:T(128)} %param.10) | copy-start | bytes 148
  146.8 1.0 copy-start.2
  150.5 8.3 collective-permute-start.1
  187.7 3.3 copy-start.10
  187.7 256.6 %copy-start.9 = (f32[4]{0:T(128)S(1)}, f32[4]{0:T(128)}, u32[]{:S(2)}) copy-start(f32[4]{0:T(128)} %param.12) | copy-start | bytes 52
  190.9 764.0 %all-reduce.7.cloned.1.call-start = ((), (), s32[]{:S(2)}) async-start(), calls=%async_computation.1 | async-start | bytes 1048576
  191.1 396.6 %copy-start.4 = (f32[4,128]{0,1:T(8,128)}, f32[4,128]{0,1:T(8,128)S(1)}, u32[]{:S(2)}) copy-start(f32[4,128]{0,1:T(8,128)S(1)} %copy.45) | copy-start | bytes 6148
  522.9 0.5 copy-start.11
  595.8 10.8 %collective-permute-start.2 = (f32[256,3,128]{2,1,0:T(4,128)}, f32[256,3,128]{2,1,0:T(4,128)S(1)}, u32[]{:S(2)}, u32[]{:S(2)}) collective-permute-start(f32[256,3,128]{2,1,0:T(4,128)} %gather_fusion.2), channel_id=1, source_target_pairs={{1,0},{2,1},{3,2},{4,3},{5,4},{6,5},{7,6},{8,7},{9,8},{10,9},{11,1... | collective-permute-start | bytes 1179656 | tf_op jit(solution)/shard_map/ppermute | solution.py:19
  640.6 6.6 copy-start.8
  655.5 1.0 copy-start.3
  657.5 8.3 collective-permute-start.3
  696.1 0.9 copy-start.1
  697.0 336.4 %copy-start.5 = (f32[4,128]{0,1:T(8,128)S(1)}, f32[4,128]{0,1:T(8,128)}, u32[]{:S(2)}) copy-start(f32[4,128]{0,1:T(8,128)} %copy-done.4) | copy-start | bytes 6148
  697.0 336.4 %copy-start.12 = (f32[128]{0:T(128)S(1)}, f32[128]{0:T(128)}, u32[]{:S(2)}) copy-start(f32[128]{0:T(128)} %copy-done.11) | copy-start | bytes 1540
Sparse Core Ops, SparseCore 0:
  191.0 253.2 all-reduce.4
  699.0 255.8 all-reduce.6
where the time goes:
time: 1050 us; the launch traced here: 1040 us
  waiting for transfers between devices  527 us (50%)
  blocking collectives  281 us (27%)
  other arithmetic  89.2 us (8%)
  local copies, waits for them, and re-layouts  67.7 us (6%)
  matrix products  55 us (5%)
  between operations  14.7 us (1%)
    unnamed x4, waiting for transfers between devices  509 us
    psum x2, blocking collectives, on_device(): squares = lax.psum(jnp.sum(update * update, axis=0), 'dom')  155 us
    all_gather x2, blocking collectives, on_device(): lax.all_gather(coef_out.astype(jnp.bfloat16), 'dom', axis=0, tiled=True)  126 us
    scatter-add x2, other arithmetic, on_device(): own_force = internal[:node_count].at[halo_nodes].add(returned)  53.1 us
    gather x2, local copies, waits for them, and re-layouts, on_device(): corner_force = element_forces(extended[connectivity], plastic, corners)  28.2 us
  transfers between devices with their start and end apart: 6, of which 6 were waited for; matrix products, arithmetic and copies ran while one was open for 1% of the time, Pallas kernels for 0%

commit v1 on v0

--- a/solution.py
+++ b/solution.py
@@ -58,7 +58,12 @@
     for sweep in range(ITERS):
         lifted = jnp.dot(
             basis,
-            lax.all_gather(coef_out.astype(jnp.bfloat16), "dom", axis=0, tiled=True),
+            jnp.concatenate(
+                lax.all_to_all(
+                    jnp.stack([coef_out.astype(jnp.bfloat16)] * lax.axis_size("dom")), "dom", 0, 0
+                ),
+                axis=0,
+            ),
             preferred_element_type=jnp.float32,
         )
         nodes = apply_scale(lifted, basis_scale).reshape(node_count, 3, cases)

time: 1050 us -> 970 us (0.924)
  blocking collectives: 281 us -> 155 us
  starting transfers between devices: 8.01 us -> 32.9 us
  waiting for transfers between devices: 527 us -> 546 us
    all_gather x2 -> x0, blocking collectives: 126 us -> none  [on_device(): lax.all_gather(coef_out.astype(jnp.bfloat16), 'dom', axis=0, tiled=True)]
    all_to_all x0 -> x2, starting transfers between devices: none -> 23.6 us  [on_device(): lax.all_to_all(jnp.stack([coef_out.astype(jnp.bfloat16)] * lax.axis_size(...]
    all_to_all x0 -> x2, waiting for transfers between devices: none -> 22.9 us  [on_device(): lax.all_to_all(jnp.stack([coef_out.astype(jnp.bfloat16)] * lax.axis_size(...]
  transfers between devices with their start and end apart: 6 -> 8, of which waited for: 6 -> 8; matrix products, arithmetic and copies ran while one was open for 1% -> 2% of each run, Pallas kernels for 0% -> 0%
where the time goes in v1:
time: 970 us; the launch traced here: 960 us
  waiting for transfers between devices  546 us (56%)
  blocking collectives  155 us (16%)
  other arithmetic  84.8 us (9%)
  local copies, waits for them, and re-layouts  69.8 us (7%)
  matrix products  55.9 us (6%)
  starting transfers between devices  32.9 us (3%)
  between operations  14.6 us (2%)
    unnamed x4, waiting for transfers between devices  504 us
    psum x2, blocking collectives, on_device(): squares = lax.psum(jnp.sum(update * update, axis=0), 'dom')  155 us
    scatter-add x2, other arithmetic, on_device(): own_force = internal[:node_count].at[halo_nodes].add(returned)  53 us
    gather x2, local copies, waits for them, and re-layouts, on_device(): corner_force = element_forces(extended[connectivity], plastic, corners)  27.8 us
    all_to_all x2, starting transfers between devices, on_device(): lax.all_to_all(jnp.stack([coef_out.astype(jnp.bfloat16)] * lax.axis_size(...  23.6 us
    all_to_all x2, waiting for transfers between devices, on_device(): lax.all_to_all(jnp.stack([coef_out.astype(jnp.bfloat16)] * lax.axis_size(...  22.9 us
  transfers between devices with their start and end apart: 8, of which 8 were waited for; matrix products, arithmetic and copies ran while one was open for 2% of the time, Pallas kernels for 0%

profile of v1, /device:TPU:1, one launch (start us, length us, event | category | flops | bytes accessed | tf_op | source)
XLA Modules:
  0.0 959.5 jit_solution(15416280364795361958)
XLA Ops:
  8.8 15.7 %all-to-all-start = ((bf16[256,4,128]{2,1,0:T(4,128)(2,1)}), bf16[256,4,128]{2,1,0:T(4,128)(2,1)S(1)}, u32[]{:S(2)}, u32[]{:S(2)}) async-start(bf16[256,4,128]{2,1,0:T(4,128)(2,1)} %stack.4), calls=%async_computation | async-start | bytes 524288 | tf_op jit(solution)/shard_map/all_to_all | solution.py:62
  31.0 8.7 all-to-all-done
  39.7 2.5 convolution_multiply_fusion
  44.5 3.0 gather_fusion
  47.5 2.6 collective-permute-start
  50.2 8.0 collective-permute-done
  58.2 2.8 pad_maximum_fusion
  61.0 13.9 %gather_fusion.1 = f32[3600,3,128]{2,1,0:T(4,128)} fusion(f32[768,3,128]{2,1,0:T(4,128)} %pad_maximum_fusion, s32[4096]{0:T(1024)S(1)} %pad_clamp_fusion), kind=kCustom, calls=%fused_computation.1 | custom fusion | bytes 11073600 | tf_op jit(solution)/shard_map/gather | solution.py:73
  75.0 8.2 fusion.6
  87.5 4.6 multiply_add_fusion.1
  92.1 6.9 convolution_bitcast_fusion.1
  99.1 8.3 fusion.1
  114.3 2.4 copy.65
  117.9 26.5 %scatter_fusion = f32[512,3,128]{2,1,0:T(4,128)} fusion(f32[512,3,128]{2,1,0:T(4,128)} %copy.65, s32[256]{0:T(256)S(1)} %copy-done.10, f32[256,3,128]{2,1,0:T(4,128)} %collective-permute-done.1), kind=kCustom, calls=%fused_computation.4 | custom fusion | flops 98304 | bytes 1180672 | tf_op jit(solution)/shard_map/scatter-add | solution.py:81
  146.7 3.2 convolution_bitcast_fusion.4
  149.9 252.2 %all-reduce.5.cloned.1.call-done = f32[1024,128]{0,1:T(8,128)} async-done(((f32[1024,128]{0,1:T(8,128)}), f32[1024,128]{0,1:T(8,128)}) %all-reduce.5.cloned.1.call-update) | async-done | bytes 524304
  403.2 77.5 %psum.14 = f32[128]{0:T(128)S(1)} all-reduce(f32[128]{0:T(128)S(1)} %multiply_reduce_fusion.3), channel_id=1, replica_groups=mesh['dom'=256] {'dom'}, use_global_device_ids=true, to_apply=%region_4.5 | all-reduce | flops 128 | bytes 1024 | tf_op jit(solution)/shard_map/psum | solution.py:93
  482.1 8.0 all-to-all-start.1
  491.1 14.2 %all-to-all-done.1 = bf16[256,4,128]{2,1,0:T(4,128)(2,1)S(1)} async-done(((bf16[256,4,128]{2,1,0:T(4,128)(2,1)}), bf16[256,4,128]{2,1,0:T(4,128)(2,1)S(1)}, u32[]{:S(2)}, u32[]{:S(2)}) %all-to-all-start.1) | async-done | bytes 262176 | tf_op jit(solution)/shard_map/all_to_all | solution.py:62
  512.0 2.8 broadcast_multiply_fusion
  514.8 3.1 gather_fusion.2
  517.9 2.6 collective-permute-start.2
  520.6 8.0 collective-permute-done.2
  528.6 2.8 pad_maximum_fusion.1
  531.5 13.9 %gather_fusion.3 = f32[3600,3,128]{2,1,0:T(4,128)} fusion(f32[768,3,128]{2,1,0:T(4,128)} %pad_maximum_fusion.1, s32[4096]{0:T(1024)S(1)} %pad_clamp_fusion), kind=kCustom, calls=%fused_computation.3 | custom fusion | bytes 11073600 | tf_op jit(solution)/shard_map/gather | solution.py:73
  545.3 8.2 fusion.4
  557.9 5.0 multiply_add_fusion
  562.9 6.4 convolution_bitcast_fusion
  569.3 8.3 fusion
  588.1 26.5 %scatter_fusion.1 = f32[512,3,128]{2,1,0:T(4,128)} fusion(f32[512,3,128]{2,1,0:T(4,128)} %copy.73, s32[256]{0:T(256)S(1)} %copy-done.10, f32[256,3,128]{2,1,0:T(4,128)} %collective-permute-done.3), kind=kCustom, calls=%fused_computation.5 | custom fusion | flops 98304 | bytes 1180672 | tf_op jit(solution)/shard_map/scatter-add | solution.py:81
  621.0 252.3 %all-reduce.7.cloned.1.call-done = f32[1024,128]{0,1:T(8,128)} async-done(((f32[1024,128]{0,1:T(8,128)}), f32[1024,128]{0,1:T(8,128)}) %all-reduce.7.cloned.1.call-update) | async-done | bytes 524304
  874.3 77.5 %psum.15 = f32[128]{0:T(128)S(1)} all-reduce(f32[128]{0:T(128)S(1)} %multiply_reduce_fusion.2), channel_id=1, replica_groups=mesh['dom'=256] {'dom'}, use_global_device_ids=true, to_apply=%region_9.10 | all-reduce | flops 128 | bytes 1024 | tf_op jit(solution)/shard_map/psum | solution.py:93
  (100 shorter events, 58.2 us)
Async XLA Ops:
  7.2 32.5 %copy-start = (bf16[1536,1024]{1,0:T(8,128)(2,1)S(1)}, bf16[1536,1024]{1,0:T(8,128)(2,1)}, u32[]{:S(2)}) copy-start(bf16[1536,1024]{1,0:T(8,128)(2,1)} %param.9) | copy-start | bytes 9437188
  8.8 30.9 %all-to-all-start = ((bf16[256,4,128]{2,1,0:T(4,128)(2,1)}), bf16[256,4,128]{2,1,0:T(4,128)(2,1)S(1)}, u32[]{:S(2)}, u32[]{:S(2)}) async-start(bf16[256,4,128]{2,1,0:T(4,128)(2,1)} %stack.4), calls=%async_computation | async-start | bytes 524288 | tf_op jit(solution)/shard_map/all_to_all | solution.py:62
  24.5 377.6 %all-reduce.5.cloned.1.call-start = ((), (), s32[]{:S(2)}) async-start(), calls=%async_computation.2 | async-start | bytes 1048576
  29.7 69.3 %copy-start.7 = (s32[3600]{0:T(1024)}, s32[3600]{0:T(1024)S(1)}, u32[]{:S(2)}) copy-start(s32[3600]{0:T(1024)S(1)} %eq.35) | copy-start | bytes 43204
  30.4 0.6 copy-start.9
  31.0 13.5 %copy-start.11 = (s32[1024]{0:T(1024)}, s32[1024]{0:T(1024)S(1)}, u32[]{:S(2)}) copy-start(s32[1024]{0:T(1024)S(1)} %pad_clamp_fusion.1) | copy-start | bytes 12292
  39.7 10.5 %copy-start.18 = (s32[450]{0:T(512)S(1)}, s32[450]{0:T(512)}, u32[]{:S(2)}) copy-start(s32[450]{0:T(512)} %param.15) | copy-start | bytes 5404
  47.5 10.7 %collective-permute-start = (f32[256,3,128]{2,1,0:T(4,128)}, f32[256,3,128]{2,1,0:T(4,128)S(1)}, u32[]{:S(2)}, u32[]{:S(2)}) collective-permute-start(f32[256,3,128]{2,1,0:T(4,128)} %gather_fusion), channel_id=1, source_target_pairs={{1,0},{2,1},{3,2},{4,3},{5,4},{6,5},{7,6},{8,7},{9,8},{10,9},{11,1... | collective-permute-start | bytes 1179656 | tf_op jit(solution)/shard_map/ppermute | solution.py:19
  50.2 37.3 %copy-start.5 = (f32[3,3]{0,1:T(4,128)}, f32[3,3]{0,1:T(4,128)S(1)}, u32[]{:S(2)}) copy-start(f32[3,3]{0,1:T(4,128)S(1)} %fusion.18) | copy-start | bytes 112
  50.2 37.2 %copy-start.16 = (pred[450]{0:T(512)(128)(4,1)}, pred[450]{0:T(512)(128)(4,1)S(1)}, u32[]{:S(2)}) copy-start(pred[450]{0:T(512)(128)(4,1)S(1)} %broadcast_compare_fusion) | copy-start | bytes 1354
  107.4 1.0 copy-start.2
  109.4 8.5 copy-start.10
  109.4 8.5 collective-permute-start.1
  146.7 256.4 %copy-start.12 = (f32[4]{0:T(128)S(1)}, f32[4]{0:T(128)}, u32[]{:S(2)}) copy-start(f32[4]{0:T(128)} %param.12) | copy-start | bytes 52
  146.7 334.0 %copy-start.14 = (f32[4,128]{1,0:T(4,128)S(1)}, f32[4,128]{1,0:T(4,128)}, u32[]{:S(2)}) copy-start(f32[4,128]{1,0:T(4,128)} %param.8) | copy-start | bytes 6148
  146.7 343.4 %copy-start.15 = (f32[12]{0:T(128)S(1)}, f32[12]{0:T(128)}, u32[]{:S(2)}) copy-start(f32[12]{0:T(128)} %param.10) | copy-start | bytes 148
  482.1 23.2 %all-to-all-start.1 = ((bf16[256,4,128]{2,1,0:T(4,128)(2,1)}), bf16[256,4,128]{2,1,0:T(4,128)(2,1)S(1)}, u32[]{:S(2)}, u32[]{:S(2)}) async-start(bf16[256,4,128]{2,1,0:T(4,128)(2,1)} %stack.5), calls=%async_computation.1 | async-start | bytes 524288 | tf_op jit(solution)/shard_map/all_to_all | solution.py:62
  490.1 383.2 %all-reduce.7.cloned.1.call-start = ((), (), s32[]{:S(2)}) async-start(), calls=%async_computation.3 | async-start | bytes 1048576
  507.3 4.7 copy-start.4
  517.9 10.7 %collective-permute-start.2 = (f32[256,3,128]{2,1,0:T(4,128)}, f32[256,3,128]{2,1,0:T(4,128)S(1)}, u32[]{:S(2)}, u32[]{:S(2)}) collective-permute-start(f32[256,3,128]{2,1,0:T(4,128)} %gather_fusion.2), channel_id=1, source_target_pairs={{1,0},{2,1},{3,2},{4,3},{5,4},{6,5},{7,6},{8,7},{9,8},{10,9},{11,1... | collective-permute-start | bytes 1179656 | tf_op jit(solution)/shard_map/ppermute | solution.py:19
  553.5 2.0 copy-start.6
  554.6 3.2 copy-start.17
  562.9 6.4 copy-start.8
  577.7 1.0 copy-start.3
  579.7 8.3 collective-permute-start.3
  618.3 0.9 copy-start.1
  619.2 332.7 %copy-start.13 = (f32[4,128]{1,0:T(4,128)S(1)}, f32[4,128]{1,0:T(4,128)}, u32[]{:S(2)}) copy-start(f32[4,128]{1,0:T(4,128)} %get-tuple-element.11) | copy-start | bytes 6148
Sparse Core Ops, SparseCore 0:
  150.0 251.9 all-reduce.4
  621.1 252.1 all-reduce.6
